TPU v7x, 32 devices: a whole 2x2x4 slice. The times are simulated.
32 devices in a mesh: seq: 8 (over z, y), head: 4 (over x, core).
Axes of the slice: x: 2, y: 2, z: 4, core: 2. Of those that a mesh axis runs over, the one named last changes fastest.
Arguments:
- queries: bfloat16 [2048, 2048], P(('seq', 'head')), may hold values from -25 to 25
- keys: bfloat16 [2048, 2048], P(('seq', 'head')), may hold values from -6 to 6
- values: bfloat16 [2048, 2048], P(('seq', 'head')), may hold values from -12 to 12
- cotangent: bfloat16 [2048, 2048], P(('seq', 'head')), may hold values from -6 to 6
- random_blocks: int32 [32, 3], P('seq'), may hold values from 0 to 31, as said below
- global_blocks: int32 [2], replicated, may hold values from 0 to 31
Outputs:
- attention_out: bfloat16 [2048, 2048], P('seq', 'head')
- grad_queries: bfloat16 [2048, 2048], P('seq', 'head')
- grad_keys: bfloat16 [2048, 2048], P('seq', 'head')
- grad_values: bfloat16 [2048, 2048], P('seq', 'head')
Inputs may be any that keep to these rules, and one draw needn't show every extreme that they name: `random_blocks`: block numbers of the document. Block c is held by seq index c // 4. Among the 12 entries of the query blocks of one seq index (aligned groups of 4 rows), at most 3 name blocks held by any one seq index; in every draw some seq index has its blocks named exactly 3 times by the entries of every seq index.
All inputs are finite; a program needn't handle non-finite values.
Results may differ from a plain program's by a relative error of at most 0.0052.
Values may be sent and summed in bfloat16 or wider, within the bound.
A program may use at most 128 MiB of HBM per device.

v0:
```python
import math

import jax
import jax.numpy as jnp
from jax import lax
from jax.sharding import PartitionSpec as P

HEAD_SIZE = 128
BLOCK_TOKENS = 64
GLOB = 2
RAND = 3


NEG_FILL = -1e30


def padded(shard, sides, width):
    for axis, dim in sides:
        size, length = (lax.axis_size(axis), shard.shape[dim])
        up = [(i, (i + 1) % size) for i in range(size - 1)]
        down = [(j, i) for i, j in up]
        last = lax.slice_in_dim(shard, length - width, length, axis=dim)
        leading = lax.slice_in_dim(shard, 0, width, axis=dim)
        before = lax.ppermute(last, axis, up)
        after = lax.ppermute(leading, axis, down)
        shard = jnp.concatenate([before, shard, after], axis=dim)
    return shard


def broadcast(block, axis, source):
    block = jnp.where(lax.axis_index(axis) == source, block, jnp.zeros_like(block))
    return lax.psum(block, axis)


def entry_ranks(owner_ids):
    count = owner_ids.shape[-1]
    earlier = jnp.arange(count)[None, :] < jnp.arange(count)[:, None]
    same_owner = owner_ids[..., :, None] == owner_ids[..., None, :]
    return jnp.sum((same_owner & earlier).astype(jnp.int32), axis=-1)


def spread_band(band_part):
    return (
        jnp.pad(band_part[:, 0], ((0, 2), (0, 0), (0, 0)))
        + jnp.pad(band_part[:, 1], ((1, 1), (0, 0), (0, 0)))
        + jnp.pad(band_part[:, 2], ((2, 0), (0, 0), (0, 0)))
    )


def shards(queries, keys, values, cotangent, random_blocks, global_blocks):
    query_rows, gathered_keys, gathered_values, cotan_rows = (
        lax.all_to_all(queries, "head", split_axis=1, concat_axis=0, tiled=True),
        lax.all_to_all(keys, "head", split_axis=1, concat_axis=0, tiled=True),
        lax.all_to_all(values, "head", split_axis=1, concat_axis=0, tiled=True),
        lax.all_to_all(cotangent, "head", split_axis=1, concat_axis=0, tiled=True),
    )
    row_count, width = query_rows.shape
    head_count = width // HEAD_SIZE
    block_count = row_count // BLOCK_TOKENS
    shard_count = lax.axis_size("seq")
    my_index = lax.axis_index("seq")
    entry_count = block_count * RAND
    slot_cap = (3 * entry_count + 2 * shard_count - 1) // (2 * shard_count)
    slot_count = shard_count * slot_cap
    key_block_sets = 3 + GLOB + RAND
    logit_scale = 1.0 / math.sqrt(HEAD_SIZE)
    key_value = jnp.stack([gathered_keys, gathered_values])
    widened = padded(key_value, (("seq", 1),), BLOCK_TOKENS)
    widened = widened.reshape(2, block_count + 2, BLOCK_TOKENS, width)
    band_rows = jnp.stack([widened[:, :-2], widened[:, 1:-1], widened[:, 2:]], axis=2)
    own_blocks = key_value.reshape(2, block_count, BLOCK_TOKENS, width)
    owner_global = global_blocks // block_count
    local_global = global_blocks % block_count
    fetched = []
    for number in range(GLOB):
        mine = jnp.take(own_blocks, local_global[number], axis=1)
        fetched.append(broadcast(mine, "seq", owner_global[number]))
    global_rows = jnp.stack(fetched, axis=1)
    entry_ids = random_blocks.reshape(entry_count)
    owner_ids = entry_ids // block_count
    slot_ids = owner_ids * slot_cap + entry_ranks(owner_ids)
    slot_hits = slot_ids[None, :] == jnp.arange(slot_count)[:, None]
    filled = jnp.any(slot_hits, axis=1)
    source = jnp.sum(jnp.where(slot_hits, jnp.arange(entry_count)[None, :], 0), axis=1)
    wanted = jnp.sum(jnp.where(slot_hits, (entry_ids % block_count)[None, :], 0), axis=1)
    asked_ids = lax.all_to_all(wanted, "seq", split_axis=0, concat_axis=0, tiled=True)
    outgoing = jnp.take(own_blocks, asked_ids, axis=1)
    incoming = lax.all_to_all(outgoing, "seq", split_axis=1, concat_axis=1, tiled=True)
    random_rows = jnp.take(incoming, slot_ids, axis=1).reshape(
        2, block_count, RAND, BLOCK_TOKENS, width
    )

    def assemble_keys(which):
        spread_global = jnp.broadcast_to(
            global_rows[which][None], (block_count, GLOB, BLOCK_TOKENS, width)
        )
        joined = jnp.concatenate([band_rows[which], spread_global, random_rows[which]], axis=1)
        return joined.reshape(block_count, key_block_sets * BLOCK_TOKENS, head_count, HEAD_SIZE)

    key_all = assemble_keys(0)
    value_all = assemble_keys(1)
    block_number = my_index * block_count + jnp.arange(block_count)
    total_blocks = shard_count * block_count
    always = jnp.ones((block_count,), dtype=bool)
    group_ok = jnp.stack(
        [block_number >= 1, always, block_number <= total_blocks - 2] + [always] * (GLOB + RAND),
        axis=1,
    )
    valid_keys = jnp.repeat(group_ok, BLOCK_TOKENS, axis=1)[:, None, None, :]
    query_blocks = query_rows.reshape(block_count, BLOCK_TOKENS, head_count, HEAD_SIZE)
    cotan_blocks = cotan_rows.reshape(block_count, BLOCK_TOKENS, head_count, HEAD_SIZE)
    score_matrix = (
        jnp.einsum("bqhd,bkhd->bhqk", query_blocks, key_all, preferred_element_type=jnp.float32)
        * logit_scale
    )
    score_matrix = jnp.where(valid_keys, score_matrix, NEG_FILL)
    row_peak = jnp.max(score_matrix, axis=-1, keepdims=True)
    exponent = jnp.exp(score_matrix - row_peak)
    weights = exponent / jnp.sum(exponent, axis=-1, keepdims=True)
    weights_low = weights.astype(jnp.bfloat16)
    attended_output = jnp.einsum(
        "bhqk,bkhd->bqhd", weights_low, value_all, preferred_element_type=jnp.float32
    ).astype(jnp.bfloat16)
    weight_gradient = jnp.einsum(
        "bqhd,bkhd->bhqk", cotan_blocks, value_all, preferred_element_type=jnp.float32
    )
    row_delta = jnp.sum(weights * weight_gradient, axis=-1, keepdims=True)
    score_grad = (weights * (weight_gradient - row_delta) * logit_scale).astype(jnp.bfloat16)
    query_gradient = jnp.einsum(
        "bhqk,bkhd->bqhd", score_grad, key_all, preferred_element_type=jnp.float32
    ).astype(jnp.bfloat16)

    def part_grads(first, count):
        low_key = first * BLOCK_TOKENS
        high_key = (first + count) * BLOCK_TOKENS
        key_part = jnp.einsum(
            "bhqk,bqhd->bkhd",
            score_grad[..., low_key:high_key],
            query_blocks,
            preferred_element_type=jnp.float32,
        )
        value_part = jnp.einsum(
            "bhqk,bqhd->bkhd",
            weights_low[..., low_key:high_key],
            cotan_blocks,
            preferred_element_type=jnp.float32,
        )
        return (
            key_part.reshape(block_count, count, BLOCK_TOKENS, width),
            value_part.reshape(block_count, count, BLOCK_TOKENS, width),
        )

    band_key, band_value = part_grads(0, 3)
    extended_key = spread_band(band_key)
    extended_value = spread_band(band_value)
    rim_pair = jnp.stack(
        [
            jnp.stack([extended_key[0], extended_key[-1]]),
            jnp.stack([extended_value[0], extended_value[-1]]),
        ]
    )
    rimmed = padded(rim_pair.astype(jnp.bfloat16), (("seq", 1),), 1).astype(rim_pair.dtype)
    key_local = extended_key[1:-1].at[0].add(rimmed[0, 0]).at[-1].add(rimmed[0, 3])
    value_local = extended_value[1:-1].at[0].add(rimmed[1, 0]).at[-1].add(rimmed[1, 3])
    global_key, global_value = part_grads(3, GLOB)
    total_key, total_value = lax.psum(
        (jnp.sum(global_key, axis=0), jnp.sum(global_value, axis=0)), "seq"
    )
    for number in range(GLOB):
        owned = owner_global[number] == my_index
        key_local = key_local.at[local_global[number]].add(jnp.where(owned, total_key[number], 0.0))
        value_local = value_local.at[local_global[number]].add(
            jnp.where(owned, total_value[number], 0.0)
        )
    random_key, random_value = part_grads(3 + GLOB, RAND)
    keep = filled[:, None, None]
    send_key = jnp.where(
        keep, jnp.take(random_key.reshape(entry_count, BLOCK_TOKENS, width), source, axis=0), 0.0
    ).astype(jnp.bfloat16)
    send_value = jnp.where(
        keep, jnp.take(random_value.reshape(entry_count, BLOCK_TOKENS, width), source, axis=0), 0.0
    ).astype(jnp.bfloat16)
    arrived_key, arrived_value = (
        lax.all_to_all(send_key, "seq", split_axis=0, concat_axis=0, tiled=True),
        lax.all_to_all(send_value, "seq", split_axis=0, concat_axis=0, tiled=True),
    )
    owner_hits = (asked_ids[None, :] == jnp.arange(block_count)[:, None]).astype(jnp.float32)
    key_local = key_local + jnp.einsum(
        "js,srf->jrf", owner_hits, arrived_key.astype(jnp.float32), precision=lax.Precision.HIGHEST
    )
    value_local = value_local + jnp.einsum(
        "js,srf->jrf",
        owner_hits,
        arrived_value.astype(jnp.float32),
        precision=lax.Precision.HIGHEST,
    )
    return (
        attended_output.reshape(row_count, width),
        query_gradient.reshape(row_count, width),
        key_local.reshape(row_count, width).astype(jnp.bfloat16),
        value_local.reshape(row_count, width).astype(jnp.bfloat16),
    )


def solution(mesh):
    in_specs = (
        P(("seq", "head"), None),
        P(("seq", "head"), None),
        P(("seq", "head"), None),
        P(("seq", "head"), None),
        P("seq", None),
        P(),
    )
    out_specs = (P("seq", "head"), P("seq", "head"), P("seq", "head"), P("seq", "head"))
    return jax.shard_map(shards, mesh=mesh, in_specs=in_specs, out_specs=out_specs, check_vma=False)
```

profile of v0, /device:TPU:11, one launch (start us, length us, event | category | flops | bytes accessed | tf_op | source)
XLA Modules:
  0.0 396.5 jit_solution(2478720990427789791)
XLA Ops:
  9.5 5.7 %all-to-all-start.2 = ((s32[8,3,1]{1,2,0:T(1,128)}), s32[8,3,1]{1,2,0:T(1,128)S(1)}, u32[]{:S(2)}, u32[]{:S(2)}) async-start(s32[8,3,1]{1,2,0:T(1,128)} %bitcast.20), calls=%async_computation.2 | async-start | bytes 8192 | tf_op jit(solution)/shard_map/all_to_all | solution.py:86
  19.2 5.7 %all-to-all-start = ((bf16[64,4,512]{2,0,1:T(8,128)(2,1)}), bf16[64,4,512]{2,0,1:T(8,128)(2,1)S(1)}, u32[]{:S(2)}, u32[]{:S(2)}) async-start(bf16[64,4,512]{2,0,1:T(8,128)(2,1)} %bitcast.229), calls=%async_computation | async-start | bytes 524288 | tf_op jit(solution)/shard_map/all_to_all | solution.py:53
  29.0 5.3 %all-to-all-start.1 = ((bf16[64,4,512]{2,0,1:T(8,128)(2,1)}), bf16[64,4,512]{2,0,1:T(8,128)(2,1)S(1)}, u32[]{:S(2)}, u32[]{:S(2)}) async-start(bf16[64,4,512]{2,0,1:T(8,128)(2,1)} %bitcast.228), calls=%async_computation.1 | async-start | bytes 524288 | tf_op jit(solution)/shard_map/all_to_all | solution.py:54
  34.3 4.1 %all-to-all-done.1 = bf16[64,4,512]{2,0,1:T(8,128)(2,1)S(1)} async-done(((bf16[64,4,512]{2,0,1:T(8,128)(2,1)}), bf16[64,4,512]{2,0,1:T(8,128)(2,1)S(1)}, u32[]{:S(2)}, u32[]{:S(2)}) %all-to-all-start.1) | async-done | bytes 262176 | tf_op jit(solution)/shard_map/all_to_all | solution.py:54
  41.0 3.9 select_bitcast_fusion
  44.9 4.9 %all-to-all-start.3 = ((bf16[2,24,64,512]{3,2,0,1:T(8,128)(2,1)}), bf16[2,24,64,512]{3,2,0,1:T(8,128)(2,1)S(1)}, u32[]{:S(2)}, u32[]{:S(2)}) async-start(bf16[2,24,64,512]{3,2,0,1:T(8,128)(2,1)} %select_bitcast_fusion), calls=%async_computation.3 | async-start | bytes 6291456 | tf_op jit(solution)/shard_map/all_to_all | solution.py:88
  53.3 3.1 collective-permute-start.1
  72.6 14.4 %collective-permute-done.1 = bf16[2,64,512]{2,1,0:T(8,128)(2,1)S(1)} collective-permute-done((bf16[2,64,512]{2,1,0:T(8,128)(2,1)}, bf16[2,64,512]{2,1,0:T(8,128)(2,1)S(1)}, u32[]{:S(2)}, u32[]{:S(2)}) %collective-permute-start.1) | collective-permute-done | bytes 131104 | tf_op jit(solution)/shard_map/ppermute | solution.py:25
  87.0 21.1 %collective-permute-done = bf16[2,64,512]{2,1,0:T(8,128)(2,1)} collective-permute-done((bf16[2,64,512]{2,1,0:T(8,128)(2,1)}, bf16[2,64,512]{2,1,0:T(8,128)(2,1)}, u32[]{:S(2)}, u32[]{:S(2)}) %collective-permute-start) | collective-permute-done | bytes 131104 | tf_op jit(solution)/shard_map/ppermute | solution.py:24
  110.7 55.2 %all-reduce.13.cloned.1.call-done = (bf16[2,1,64,512]{3,2,0,1:T(8,128)(2,1)}, bf16[2,1,64,512]{3,2,0,1:T(8,128)(2,1)}) async-done(((bf16[2,1,64,512]{3,2,0,1:T(8,128)(2,1)}, bf16[2,1,64,512]{3,2,0,1:T(8,128)(2,1)}), (bf16[2,1,64,512]{3,2,0,1:T(8,128)(2,1)}, bf16[2,1,64,512]{3,2,0,1:T(8,128)(2,1)})) %all-reduce.13.cloned.1.call-update) | async-done | bytes 262160 | tf_op jit(solution)/shard_map/psum | solution.py:32
  168.4 6.0 %all-to-all-start.4 = ((bf16[64,4,512]{2,0,1:T(8,128)(2,1)}), bf16[64,4,512]{2,0,1:T(8,128)(2,1)S(1)}, u32[]{:S(2)}, u32[]{:S(2)}) async-start(bf16[64,4,512]{2,0,1:T(8,128)(2,1)} %bitcast.241), calls=%async_computation.4 | async-start | bytes 524288 | tf_op jit(solution)/shard_map/all_to_all | solution.py:52
  187.8 3.9 reshape.539
  191.8 3.6 all-to-all-start.5
  202.4 6.7 %fusion.6 = bf16[4,4,64,512]{3,2,1,0:T(8,128)(2,1)} fusion(f32[4,4,512,64]{2,3,1,0:T(8,128)S(1)} %fusion.11, f32[4,4,64,512]{3,2,1,0:T(8,128)S(1)} %copy-done.8, f32[4,4,64]{2,1,0:T(4,128)S(1)} %get-tuple-element.166), kind=kOutput, calls=%fused_computation.17 | output fusion | flops 3671551 | bytes 5246976 | tf_op jit(solution)/shard_map/sub | solution.py:128
  220.6 3.1 gather_fusion.2
  223.7 4.8 %fusion.2 = (bf16[24,64,512]{2,1,0:T(8,128)(2,1)}, bf16[24,64,512]{2,1,0:T(8,128)(2,1)}) fusion(bf16[24,64,512]{2,1,0:T(8,128)(2,1)} %gather_fusion.3, pred[24]{0:T(512)(128)(4,1)S(1)} %copy-done.17, pred[24]{0:T(512)(128)(4,1)S(1)} %copy-done.16, bf16[24,64,512]{2,1,0:T(8,128)(2,1)} %gather_fusion.2), kind=kLoop, calls=%fused_computation.7 | loop fusion | flops 3145728 | bytes 6291504 | tf_op jit(solution)/shard_map/convert_element_type | solution.py:182
  228.5 5.1 %all-to-all-start.6 = ((bf16[24,64,512]{2,1,0:T(8,128)(2,1)}), bf16[24,64,512]{2,1,0:T(8,128)(2,1)}, u32[]{:S(2)}, u32[]{:S(2)}) async-start(bf16[24,64,512]{2,1,0:T(8,128)(2,1)} %get-tuple-element.157), calls=%async_computation.6 | async-start | bytes 3145728 | tf_op jit(solution)/shard_map/all_to_all | solution.py:184
  254.2 9.8 %fusion.44 = bf16[4,64,4,128]{3,1,2,0:T(8,128)(2,1)} fusion(bf16[4,512,4,128]{3,2,1,0:T(4,128)(2,1)S(1)} %reshape.540, f32[4,4,512,64]{2,3,1,0:T(8,128)} %copy-done.9, f32[4,4,64,512]{3,2,1,0:T(8,128)} %copy-done.7, f32[4,4,64]{2,1,0:T(4,128)S(1)} %get-tuple-element.166), kind=kOutput, calls=%fused_computation.50 | convolution fusion | flops 138020352 | bytes 6557696 | tf_op jit(solution)/shard_map/bhqk,bkhd->bqhd/dot_general | solution.py:129
  264.0 3.1 fusion.41
  268.9 5.7 %all-to-all-start.7 = ((bf16[24,64,512]{2,1,0:T(8,128)(2,1)}), bf16[24,64,512]{2,1,0:T(8,128)(2,1)S(1)}, u32[]{:S(2)}, u32[]{:S(2)}) async-start(bf16[24,64,512]{2,1,0:T(8,128)(2,1)} %get-tuple-element.156), calls=%async_computation.7 | async-start | bytes 3145728 | tf_op jit(solution)/shard_map/all_to_all | solution.py:185
  280.7 3.1 collective-permute-start.3
  293.5 4.4 %collective-permute-done.3 = bf16[2,1,64,512]{3,1,2,0:T(2,128)(2,1)} collective-permute-done((bf16[2,1,64,512]{3,1,2,0:T(2,128)(2,1)}, bf16[2,1,64,512]{3,1,2,0:T(2,128)(2,1)}, u32[]{:S(2)}, u32[]{:S(2)}) %collective-permute-start.3) | collective-permute-done | bytes 131104 | tf_op jit(solution)/shard_map/ppermute | solution.py:25
  297.9 12.1 %collective-permute-done.2 = bf16[2,1,64,512]{3,1,2,0:T(2,128)(2,1)} collective-permute-done((bf16[2,1,64,512]{3,1,2,0:T(2,128)(2,1)}, bf16[2,1,64,512]{3,1,2,0:T(2,128)(2,1)}, u32[]{:S(2)}, u32[]{:S(2)}) %collective-permute-start.2) | collective-permute-done | bytes 131104 | tf_op jit(solution)/shard_map/ppermute | solution.py:24
  321.3 50.8 %all-reduce.11.cloned.1.call-done = (f32[2,64,512]{2,0,1:T(2,128)}, f32[2,64,512]{2,0,1:T(2,128)}) async-done(((f32[2,64,512]{2,0,1:T(2,128)}, f32[2,64,512]{2,0,1:T(2,128)}), (f32[2,64,512]{2,0,1:T(2,128)}, f32[2,64,512]{2,0,1:T(2,128)})) %all-reduce.11.cloned.1.call-update) | async-done | bytes 524304 | tf_op jit(solution)/shard_map/psum | solution.py:166
  (165 shorter events, 130.1 us)
Async XLA Ops:
  9.5 9.8 %all-to-all-start.2 = ((s32[8,3,1]{1,2,0:T(1,128)}), s32[8,3,1]{1,2,0:T(1,128)S(1)}, u32[]{:S(2)}, u32[]{:S(2)}) async-start(s32[8,3,1]{1,2,0:T(1,128)} %bitcast.20), calls=%async_computation.2 | async-start | bytes 8192 | tf_op jit(solution)/shard_map/all_to_all | solution.py:86
  19.2 9.8 %all-to-all-start = ((bf16[64,4,512]{2,0,1:T(8,128)(2,1)}), bf16[64,4,512]{2,0,1:T(8,128)(2,1)S(1)}, u32[]{:S(2)}, u32[]{:S(2)}) async-start(bf16[64,4,512]{2,0,1:T(8,128)(2,1)} %bitcast.229), calls=%async_computation | async-start | bytes 524288 | tf_op jit(solution)/shard_map/all_to_all | solution.py:53
  29.0 9.4 %all-to-all-start.1 = ((bf16[64,4,512]{2,0,1:T(8,128)(2,1)}), bf16[64,4,512]{2,0,1:T(8,128)(2,1)S(1)}, u32[]{:S(2)}, u32[]{:S(2)}) async-start(bf16[64,4,512]{2,0,1:T(8,128)(2,1)} %bitcast.228), calls=%async_computation.1 | async-start | bytes 524288 | tf_op jit(solution)/shard_map/all_to_all | solution.py:54
  44.9 4.9 %copy-start.12 = (s32[4,3]{1,0:T(4,128)S(1)}, s32[4,3]{1,0:T(4,128)}, u32[]{:S(2)}) copy-start(s32[4,3]{1,0:T(4,128)} %param.30) | copy-start | bytes 148
  44.9 5.0 %copy-start.18 = (s32[2]{0:T(128)S(1)}, s32[2]{0:T(128)}, u32[]{:S(2)}) copy-start(s32[2]{0:T(128)} %param.31) | copy-start | bytes 28
  44.9 123.6 %all-to-all-start.3 = ((bf16[2,24,64,512]{3,2,0,1:T(8,128)(2,1)}), bf16[2,24,64,512]{3,2,0,1:T(8,128)(2,1)S(1)}, u32[]{:S(2)}, u32[]{:S(2)}) async-start(bf16[2,24,64,512]{3,2,0,1:T(8,128)(2,1)} %select_bitcast_fusion), calls=%async_computation.3 | async-start | bytes 6291456 | tf_op jit(solution)/shard_map/all_to_all | solution.py:88
  49.8 116.2 %all-reduce.13.cloned.1.call-start = ((), (), s32[]{:S(2)}) async-start(), calls=%async_computation.9 | async-start | bytes 524288 | tf_op jit(solution)/shard_map/psum | solution.py:32
  53.3 33.7 %collective-permute-start.1 = (bf16[2,64,512]{2,1,0:T(8,128)(2,1)}, bf16[2,64,512]{2,1,0:T(8,128)(2,1)S(1)}, u32[]{:S(2)}, u32[]{:S(2)}) collective-permute-start(bf16[2,64,512]{2,1,0:T(8,128)(2,1)} %get-tuple-element.149), channel_id=1, source_target_pairs={{4,0},{8,4},{12,8},{16,12},{20,16},{24,20},{28,24},{5,1},{9,5},{13... | collective-permute-start | bytes 393224 | tf_op jit(solution)/shard_map/ppermute | solution.py:25
  56.4 51.7 %collective-permute-start = (bf16[2,64,512]{2,1,0:T(8,128)(2,1)}, bf16[2,64,512]{2,1,0:T(8,128)(2,1)}, u32[]{:S(2)}, u32[]{:S(2)}) collective-permute-start(bf16[2,64,512]{2,1,0:T(8,128)(2,1)} %get-tuple-element.148), channel_id=1, source_target_pairs={{0,4},{4,8},{8,12},{12,16},{16,20},{20,24},{24,28},{1,5},{5,9},{9,... | collective-permute-start | bytes 393224 | tf_op jit(solution)/shard_map/ppermute | solution.py:24
  168.4 23.3 %all-to-all-start.4 = ((bf16[64,4,512]{2,0,1:T(8,128)(2,1)}), bf16[64,4,512]{2,0,1:T(8,128)(2,1)S(1)}, u32[]{:S(2)}, u32[]{:S(2)}) async-start(bf16[64,4,512]{2,0,1:T(8,128)(2,1)} %bitcast.241), calls=%async_computation.4 | async-start | bytes 524288 | tf_op jit(solution)/shard_map/all_to_all | solution.py:52
  182.3 2.7 copy-start.3
  191.8 8.0 %all-to-all-start.5 = ((bf16[64,4,512]{2,0,1:T(8,128)(2,1)}), bf16[64,4,512]{2,0,1:T(8,128)(2,1)S(1)}, u32[]{:S(2)}, u32[]{:S(2)}) async-start(bf16[64,4,512]{2,0,1:T(8,128)(2,1)} %bitcast.226), calls=%async_computation.5 | async-start | bytes 524288 | tf_op jit(solution)/shard_map/all_to_all | solution.py:55
  202.4 6.8 %copy-start.9 = (f32[4,4,512,64]{2,3,1,0:T(8,128)}, f32[4,4,512,64]{2,3,1,0:T(8,128)S(1)}, u32[]{:S(2)}) copy-start(f32[4,4,512,64]{2,3,1,0:T(8,128)S(1)} %fusion.11) | copy-start | bytes 6291460
  202.4 6.8 %copy-start.2 = (bf16[4,4,64,512]{3,2,1,0:T(8,128)(2,1)S(1)}, bf16[4,4,64,512]{3,2,1,0:T(8,128)(2,1)}, u32[]{:S(2)}) copy-start(bf16[4,4,64,512]{3,2,1,0:T(8,128)(2,1)} %fusion.102) | copy-start | bytes 3145732
  220.6 3.1 copy-start.16
  220.6 3.1 copy-start.17
  228.5 6.4 %copy-start.15 = (s32[3]{0:T(128)S(1)}, s32[3]{0:T(128)}, u32[]{:S(2)}) copy-start(s32[3]{0:T(128)} %constant.293.clone.1) | copy-start | bytes 40
  228.5 40.4 %all-to-all-start.6 = ((bf16[24,64,512]{2,1,0:T(8,128)(2,1)}), bf16[24,64,512]{2,1,0:T(8,128)(2,1)}, u32[]{:S(2)}, u32[]{:S(2)}) async-start(bf16[24,64,512]{2,1,0:T(8,128)(2,1)} %get-tuple-element.157), calls=%async_computation.6 | async-start | bytes 3145728 | tf_op jit(solution)/shard_map/all_to_all | solution.py:184
  268.9 8.1 %copy-start.11 = (bf16[4,64,4,128]{3,1,2,0:T(8,128)(2,1)S(1)}, bf16[4,64,4,128]{3,1,2,0:T(8,128)(2,1)}, u32[]{:S(2)}) copy-start(bf16[4,64,4,128]{3,1,2,0:T(8,128)(2,1)} %fusion.44) | copy-start | bytes 786436
  268.9 118.9 %all-to-all-start.7 = ((bf16[24,64,512]{2,1,0:T(8,128)(2,1)}), bf16[24,64,512]{2,1,0:T(8,128)(2,1)S(1)}, u32[]{:S(2)}, u32[]{:S(2)}) async-start(bf16[24,64,512]{2,1,0:T(8,128)(2,1)} %get-tuple-element.156), calls=%async_computation.7 | async-start | bytes 3145728 | tf_op jit(solution)/shard_map/all_to_all | solution.py:185
  274.6 97.5 %all-reduce.11.cloned.1.call-start = ((), (), s32[]{:S(2)}) async-start(), calls=%async_computation.8 | async-start | bytes 1048576 | tf_op jit(solution)/shard_map/psum | solution.py:166
  274.9 11.4 %copy-start.5 = (f32[6,64,512]{2,0,1:T(8,128)S(1)}, f32[6,64,512]{2,0,1:T(8,128)}, u32[]{:S(2)}) copy-start(f32[6,64,512]{2,0,1:T(8,128)} %get-tuple-element.124) | copy-start | bytes 2359300
  280.7 17.2 %collective-permute-start.3 = (bf16[2,1,64,512]{3,1,2,0:T(2,128)(2,1)}, bf16[2,1,64,512]{3,1,2,0:T(2,128)(2,1)}, u32[]{:S(2)}, u32[]{:S(2)}) collective-permute-start(bf16[2,1,64,512]{3,1,2,0:T(2,128)(2,1)} %get-tuple-element.153), channel_id=1, source_target_pairs={{4,0},{8,4},{12,8},{16,12},{20,16},{24,20},{28,24},{5,1},{9,5},{13... | collective-permute-start | bytes 393224 | tf_op jit(solution)/shard_map/ppermute | solution.py:25
  283.8 26.2 %collective-permute-start.2 = (bf16[2,1,64,512]{3,1,2,0:T(2,128)(2,1)}, bf16[2,1,64,512]{3,1,2,0:T(2,128)(2,1)}, u32[]{:S(2)}, u32[]{:S(2)}) collective-permute-start(bf16[2,1,64,512]{3,1,2,0:T(2,128)(2,1)} %get-tuple-element.152), channel_id=1, source_target_pairs={{0,4},{4,8},{8,12},{12,16},{16,20},{20,24},{24,28},{1,5},{5,9},{9,... | collective-permute-start | bytes 393224 | tf_op jit(solution)/shard_map/ppermute | solution.py:24
  (9 other events, 16.4 us)
Sparse Core Ops, SparseCore 0:
  72.8 93.1 all-reduce.12
  293.6 78.3 all-reduce.10
where the time goes:
time: 402 us; the launch traced here: 397 us
  waiting for transfers between devices  167 us (42%)
  local copies, waits for them, and re-layouts  80.9 us (20%)
  starting transfers between devices  52.7 us (13%)
  other arithmetic  45.9 us (11%)
  matrix products  28.6 us (7%)
  between operations  21.1 us (5%)
    psum x1, waiting for transfers between devices, broadcast(): return lax.psum(block, axis)  55.2 us
    psum x1, waiting for transfers between devices, shards(): lax.psum((jnp.sum(global_key, axis=0), jnp.sum(global_value, axis=0)), 's...  50.8 us
    ppermute x2, waiting for transfers between devices, padded(): before = lax.ppermute(last, axis, up)  33.1 us
    ppermute x2, waiting for transfers between devices, padded(): after = lax.ppermute(leading, axis, down)  18.8 us
    another operation x7, other arithmetic  10.7 us
    dot_general x1, matrix products, shards(): jnp.einsum('bhqk,bkhd->bqhd', score_grad, key_all, preferred_element_type...  9.77 us
  transfers between devices with their start and end apart: 14, of which 10 were waited for; matrix products, arithmetic and copies ran while one was open for 29% of the time, Pallas kernels for 0%

commit v1 on v0

--- a/solution.py
+++ b/solution.py
@@ -1,8 +1,11 @@
+import functools
 import math
 
 import jax
 import jax.numpy as jnp
 from jax import lax
+from jax.experimental import pallas as pl
+from jax.experimental.pallas import tpu as pltpu
 from jax.sharding import PartitionSpec as P
 
 HEAD_SIZE = 128
@@ -202,6 +205,301 @@
     )
 
 
+MESH = pl.DeviceIdType.MESH
+GROUP = 4
+
+
+def contract(a, b, dim_a, dim_b):
+    return lax.dot_general(
+        a, b, (((dim_a,), (dim_b,)), ((), ())), preferred_element_type=jnp.float32
+    )
+
+
+def head_kernel(
+    seq, heads, per_out,
+    k_ref, q_ref, v_ref, g_ref, random_ref, global_ref,
+    out_ref, dq_ref, dk_ref, dv_ref,
+    kb, qb, vb, gb, cb, bias, dka, dva, dkr, dvr, stage,
+    send_sem, recv_sem, own_sem, swap_send, swap_recv, grad_send, grad_recv,
+    out_send, out_recv,
+):
+    s = lax.axis_index("seq")
+    h = lax.axis_index("head")
+    x, c = h // 2, h % 2
+    planes = heads // 2
+    chips = seq * planes
+    devices = seq * heads
+    me = s * heads + h
+    place = s * planes + x
+    sources = (k_ref, q_ref, v_ref, g_ref)
+    landing = (kb.at[c], qb, vb.at[c], gb)
+    sibling = (s, 2 * x + 1 - c)
+
+    barrier = pltpu.get_barrier_semaphore()
+
+    @pl.loop(1, devices)
+    def _(j):
+        to = (me + j) % devices
+        pl.semaphore_signal(
+            barrier, inc=1, device_id=(to // heads, to % heads), device_id_type=MESH
+        )
+
+    lane = lax.broadcasted_iota(jnp.int32, (8, 128), 1)
+    block = jnp.where(lane < chips, 2 * lane, 2 * (lane - chips) + 1)
+    block = jnp.where(lane < 2 * chips, block, -9)
+    mine = s * heads + h
+    entries = [mine - 1, mine, mine + 1]
+    entries += [global_ref[e] for e in range(GLOB)]
+    entries += [random_ref[h, e] for e in range(RAND)]
+    count = jnp.zeros((8, 128), jnp.float32)
+    for entry in entries:
+        count = count + jnp.where(block == entry, 1.0, 0.0)
+    cb[place] = count
+
+    pl.semaphore_wait(barrier, devices - 1)
+
+    def columns(to_s, to_x):
+        return pl.ds(pl.multiple_of((seq * to_x + to_s) * HEAD_SIZE, HEAD_SIZE), HEAD_SIZE)
+
+    def block_copy(a, j):
+        to = (place + j) % chips
+        to_s, to_x = to // planes, to % planes
+        if a < 4:
+            src, dst = sources[a].at[:, columns(to_s, to_x)], landing[a].at[place]
+        else:
+            src, dst = cb.at[place], cb.at[place]
+        return pltpu.make_async_remote_copy(
+            src_ref=src, dst_ref=dst, send_sem=send_sem.at[a, j], recv_sem=recv_sem.at[a, place],
+            device_id=(to_s, 2 * to_x + c), device_id_type=MESH,
+        )
+
+    def arrival(a, p):
+        ref = landing[a].at[p] if a < 4 else cb.at[p]
+        return pltpu.make_async_remote_copy(
+            src_ref=ref, dst_ref=ref, send_sem=send_sem.at[a, 0], recv_sem=recv_sem.at[a, p],
+            device_id=sibling, device_id_type=MESH,
+        )
+
+    own = [
+        pltpu.make_async_copy(
+            sources[a].at[:, columns(s, x)], landing[a].at[place], own_sem.at[a]
+        )
+        for a in range(4)
+    ]
+    for a in range(4):
+        own[a].start()
+    for group in ((0, 4, 1), (2, 3)):
+        @pl.loop(1, chips)
+        def _(j):
+            for a in group:
+                block_copy(a, j).start()
+    for a in range(4):
+        own[a].wait()
+
+    def swap(n, part):
+        ref = (kb, vb)[n].at[part]
+        return pltpu.make_async_remote_copy(
+            src_ref=ref, dst_ref=ref, send_sem=swap_send.at[n], recv_sem=swap_recv.at[n],
+            device_id=sibling, device_id_type=MESH,
+        )
+
+    def arrive(a):
+        @pl.loop(1, chips)
+        def _(j):
+            arrival(a, (place + j) % chips).wait_recv()
+
+    arrive(0)
+    swap(0, c).start()
+    arrive(4)
+    arrive(1)
+
+    rows = lax.broadcasted_iota(jnp.int32, (8 * chips, chips * BLOCK_TOKENS), 0)
+    cols = lax.broadcasted_iota(jnp.int32, (8 * chips, chips * BLOCK_TOKENS), 1)
+    spread = jnp.where(rows == 8 * (cols // BLOCK_TOKENS), 1.0, 0.0)
+    counts = contract(cb[...].reshape(8 * chips, 128), spread, 0, 0)[: 2 * chips]
+    logs = jnp.where(counts > 0.5, jnp.log(jnp.maximum(counts, 1.0)), NEG_FILL)
+    width = GROUP * BLOCK_TOKENS
+    for u in range(chips // GROUP):
+        bias[u] = logs[:, u * width : (u + 1) * width]
+
+    arrive(2)
+    swap(1, c).start()
+    arrive(3)
+    dka[...] = jnp.zeros_like(dka)
+    dva[...] = jnp.zeros_like(dva)
+    swap(0, 1 - c).wait_recv()
+    swap(1, 1 - c).wait_recv()
+
+    total = 2 * chips * BLOCK_TOKENS
+    scale = 1.0 / math.sqrt(HEAD_SIZE)
+
+    @pl.loop(0, chips // GROUP)
+    def _(u):
+        picked = pl.ds(u * GROUP, GROUP)
+        keys = kb[...].reshape(total, HEAD_SIZE)
+        values = vb[...].reshape(total, HEAD_SIZE)
+        query = qb[picked].reshape(width, HEAD_SIZE)
+        cotan = gb[picked].reshape(width, HEAD_SIZE)
+        score = contract(keys, query, 1, 1).reshape(2 * chips, BLOCK_TOKENS, width)
+        score = (score * scale + bias[u][:, None, :]).reshape(total, width)
+        power = jnp.exp(score - jnp.max(score, axis=0, keepdims=True))
+        prob = power * (1.0 / jnp.sum(power, axis=0, keepdims=True))
+        low = prob.astype(jnp.bfloat16)
+        dprob = contract(values, cotan, 1, 1)
+        delta = jnp.sum(prob * dprob, axis=0, keepdims=True)
+        dscore = (prob * (dprob - delta) * scale).astype(jnp.bfloat16)
+        attended = contract(low, values, 0, 0)
+        dquery = contract(dscore, keys, 0, 0)
+        halves = (GROUP // planes, planes, BLOCK_TOKENS, HEAD_SIZE)
+        slot = pl.ds(u * (GROUP // planes), GROUP // planes)
+        stage[0, slot] = attended.astype(jnp.bfloat16).reshape(halves)
+        stage[1, slot] = dquery.astype(jnp.bfloat16).reshape(halves)
+        dka[...] += contract(dscore, query, 1, 0).reshape(dka.shape)
+        dva[...] += contract(low, cotan, 1, 0).reshape(dva.shape)
+
+    def grad_copy(n):
+        return pltpu.make_async_remote_copy(
+            src_ref=(dka, dva)[n].at[1 - c], dst_ref=(dkr, dvr)[n],
+            send_sem=grad_send.at[n], recv_sem=grad_recv.at[n],
+            device_id=sibling, device_id_type=MESH,
+        )
+
+    grad_copy(0).start()
+    grad_copy(1).start()
+
+    results = (out_ref, dq_ref, dk_ref, dv_ref)
+    out_core, out_slot = s // per_out, s % per_out
+
+    def out_copy(a, t):
+        lanes = pl.ds(pl.multiple_of(out_slot * HEAD_SIZE, HEAD_SIZE), HEAD_SIZE)
+        return pltpu.make_async_remote_copy(
+            src_ref=stage.at[a, t], dst_ref=results[a].at[:, c, :, lanes],
+            send_sem=out_send.at[a, t], recv_sem=out_recv.at[a, out_slot, c],
+            device_id=(t, 2 * x + out_core), device_id_type=MESH,
+        )
+
+    def out_own(a):
+        lanes = pl.ds(pl.multiple_of(out_slot * HEAD_SIZE, HEAD_SIZE), HEAD_SIZE)
+        return pltpu.make_async_copy(
+            stage.at[a, s], results[a].at[:, c, :, lanes], own_sem.at[a]
+        )
+
+    keep = out_core == c
+
+    def send_out(a):
+        @pl.loop(1, seq)
+        def _(j):
+            out_copy(a, (s + j) % seq).start()
+
+        @pl.when(keep)
+        def _():
+            out_own(a).start()
+
+        @pl.when(jnp.logical_not(keep))
+        def _():
+            out_copy(a, s).start()
+
+    send_out(0)
+    send_out(1)
+    for n in range(2):
+        grad_copy(n).wait_recv()
+        final = (dka, dva)[n][c] + (dkr, dvr)[n][...]
+        stage[2 + n] = final.astype(jnp.bfloat16).reshape(stage.shape[1:])
+        send_out(2 + n)
+
+    for a in range(5):
+        @pl.loop(1, chips)
+        def _(j):
+            block_copy(a, j).wait_send()
+    for n in range(2):
+        swap(n, c).wait_send()
+        grad_copy(n).wait_send()
+    for a in range(4):
+        @pl.loop(1, seq)
+        def _(j):
+            out_copy(a, (s + j) % seq).wait_send()
+
+        @pl.when(keep)
+        def _():
+            out_own(a).wait()
+
+        @pl.when(jnp.logical_not(keep))
+        def _():
+            out_copy(a, s).wait_send()
+
+        for d in range(per_out):
+            for core in range(2):
+                @pl.when(jnp.logical_not((s == c * per_out + d) & (core == c)))
+                def _():
+                    lanes = pl.ds(d * HEAD_SIZE, HEAD_SIZE)
+                    ref = results[a].at[:, core, :, lanes]
+                    pltpu.make_async_remote_copy(
+                        src_ref=stage.at[a, 0], dst_ref=ref, send_sem=out_send.at[a, 0],
+                        recv_sem=out_recv.at[a, d, core],
+                        device_id=sibling, device_id_type=MESH,
+                    ).wait_recv()
+
+
+def by_head(seq, heads, queries, keys, values, cotangent, random_blocks, global_blocks):
+    rows, feat = queries.shape
+    planes = heads // 2
+    chips = seq * planes
+    per_out = feat // HEAD_SIZE // heads
+    half = chips * rows
+    low, wide = jnp.bfloat16, jnp.float32
+    dma = pltpu.SemaphoreType.DMA
+    shape = jax.ShapeDtypeStruct((planes, 2, rows, per_out * HEAD_SIZE), low)
+    blocks = (chips, rows, HEAD_SIZE)
+    flops = 6 * 2 * half * 2 * half * HEAD_SIZE
+    results = pl.pallas_call(
+        functools.partial(head_kernel, seq, heads, per_out),
+        out_shape=[shape] * 4,
+        in_specs=[pl.BlockSpec(memory_space=pl.ANY)] * 4
+        + [pl.BlockSpec(memory_space=pltpu.SMEM)] * 2,
+        out_specs=[pl.BlockSpec(memory_space=pl.ANY)] * 4,
+        scratch_shapes=[
+            pltpu.VMEM((2,) + blocks, low),
+            pltpu.VMEM(blocks, low),
+            pltpu.VMEM((2,) + blocks, low),
+            pltpu.VMEM(blocks, low),
+            pltpu.VMEM((chips, 8, 128), wide),
+            pltpu.VMEM((chips // GROUP, 2 * chips, GROUP * rows), wide),
+            pltpu.VMEM((2, half, HEAD_SIZE), wide),
+            pltpu.VMEM((2, half, HEAD_SIZE), wide),
+            pltpu.VMEM((half, HEAD_SIZE), wide),
+            pltpu.VMEM((half, HEAD_SIZE), wide),
+            pltpu.VMEM((4, seq, planes, rows, HEAD_SIZE), low),
+            dma((5, chips)),
+            dma((5, chips)),
+            dma((4,)),
+            dma((2,)),
+            dma((2,)),
+            dma((2,)),
+            dma((2,)),
+            dma((4, seq)),
+            dma((4, per_out, 2)),
+        ],
+        compiler_params=pltpu.CompilerParams(
+            collective_id=0, has_side_effects=True, vmem_limit_bytes=48 * 2**20
+        ),
+        cost_estimate=pl.CostEstimate(
+            flops=flops, bytes_accessed=16 * rows * feat, transcendentals=2 * half * half
+        ),
+    )(keys, queries, values, cotangent, random_blocks, global_blocks)
+    return tuple(r.reshape(2 * planes * rows, per_out * HEAD_SIZE) for r in results)
+
+
+def shards_or_heads(queries, keys, values, cotangent, random_blocks, global_blocks):
+    seq, heads = lax.axis_size("seq"), lax.axis_size("head")
+    rows, feat = queries.shape
+    count = feat // HEAD_SIZE
+    one_each = heads == 4 and 2 * count == seq * heads and rows == BLOCK_TOKENS
+    args = (queries, keys, values, cotangent, random_blocks, global_blocks)
+    if one_each and seq == 2 * (count // heads):
+        return by_head(seq, heads, *args)
+    return shards(*args)
+
+
 def solution(mesh):
     in_specs = (
         P(("seq", "head"), None),
@@ -212,4 +510,6 @@
         P(),
     )
     out_specs = (P("seq", "head"), P("seq", "head"), P("seq", "head"), P("seq", "head"))
-    return jax.shard_map(shards, mesh=mesh, in_specs=in_specs, out_specs=out_specs, check_vma=False)
+    return jax.shard_map(
+        shards_or_heads, mesh=mesh, in_specs=in_specs, out_specs=out_specs, check_vma=False
+    )

time: 402 us -> 78.6 us (0.20); the launches traced: 397 us -> 77.2 us
  waiting for transfers between devices: 167 us -> 0 us
  local copies, waits for them, and re-layouts: 80.9 us -> 7.94 us
  Pallas kernels: 0 us -> 68.6 us
  starting transfers between devices: 52.7 us -> 0 us
  other arithmetic: 45.9 us -> 0 us
  matrix products: 28.6 us -> 0 us
  between operations: 21.1 us -> 0.66 us
    psum x2 -> x0, waiting for transfers between devices: 106 us -> none  [the longest x1 55.2 us: broadcast(): return lax.psum(block, axis)]
    pallas_call x0 -> x1, Pallas kernels: none -> 68.6 us  [by_head(): pl.pallas_call(functools.partial(head_kernel, seq, heads, per_out), out_s...]
    ppermute x4 -> x0, waiting for transfers between devices: 51.9 us -> none  [the longest x2 33.1 us: padded(): before = lax.ppermute(last, axis, up)]
    all_to_all x8 -> x0, starting transfers between devices: 41.9 us -> none  [the longest x1 6.01 us: shards(): lax.all_to_all(queries, 'head', split_axis=1, concat_axis=0, tiled=True)]
    dot_general x12 -> x0, matrix products: 28.6 us -> none  [the longest x1 9.77 us: shards(): jnp.einsum('bhqk,bkhd->bqhd', score_grad, key_all, preferred_element_type...]
    reshape x8 -> x0, local copies, waits for them, and re-layouts: 17.7 us -> none  [the longest x2 6.57 us: assemble_keys(): joined.reshape(block_count, key_block_sets * BLOCK_TOKENS, head_count, HE...]
    another operation x13 -> x0, other arithmetic: 14.3 us -> none
    ppermute x4 -> x0, starting transfers between devices: 10.8 us -> none  [the longest x2 6.15 us: padded(): after = lax.ppermute(leading, axis, down)]
  transfers between devices with their start and end apart: 14 -> 0, of which waited for: 10 -> 0; matrix products, arithmetic and copies ran while one was open for 29% -> 0% of each run, Pallas kernels for 0% -> 0%
where the time goes in v1:
time: 78.6 us; the launch traced here: 77.2 us
  Pallas kernels  68.6 us (87%)
  local copies, waits for them, and re-layouts  7.94 us (10%)
    pallas_call x1, Pallas kernels, by_head(): pl.pallas_call(functools.partial(head_kernel, seq, heads, per_out), out_s...  68.6 us
    unnamed x16, local copies, waits for them, and re-layouts  7.94 us

profile of v1, /device:TPU:11, one launch (start us, length us, event | category | flops | bytes accessed | tf_op | source)
XLA Modules:
  0.0 77.2 jit_solution(14844178971986789006)
XLA Ops:
  0.6 0.0 copy-start
  0.6 0.9 %copy-done = bf16[64,2048]{1,0:T(8,128)(2,1)S(1)} copy-done((bf16[64,2048]{1,0:T(8,128)(2,1)S(1)}, bf16[64,2048]{1,0:T(8,128)(2,1)}, u32[]{:S(2)}) %copy-start) | copy-done | bytes 262168
  1.6 0.0 copy-start.1
  1.6 0.9 %copy-done.1 = bf16[64,2048]{1,0:T(8,128)(2,1)S(1)} copy-done((bf16[64,2048]{1,0:T(8,128)(2,1)S(1)}, bf16[64,2048]{1,0:T(8,128)(2,1)}, u32[]{:S(2)}) %copy-start.1) | copy-done | bytes 262168
  2.5 0.0 copy-start.2
  2.5 0.9 %copy-done.2 = bf16[64,2048]{1,0:T(8,128)(2,1)S(1)} copy-done((bf16[64,2048]{1,0:T(8,128)(2,1)S(1)}, bf16[64,2048]{1,0:T(8,128)(2,1)}, u32[]{:S(2)}) %copy-start.2) | copy-done | bytes 262168
  3.5 0.0 copy-start.3
  3.5 0.9 %copy-done.3 = bf16[64,2048]{1,0:T(8,128)(2,1)S(1)} copy-done((bf16[64,2048]{1,0:T(8,128)(2,1)S(1)}, bf16[64,2048]{1,0:T(8,128)(2,1)}, u32[]{:S(2)}) %copy-start.3) | copy-done | bytes 262168
  4.4 0.0 copy-start.4
  4.4 0.7 copy-done.4
  5.1 0.0 copy-start.5
  5.1 0.7 copy-done.5
  5.8 68.6 %shard_map.93 = (bf16[2,2,64,512]{3,2,1,0:T(8,128)(2,1)S(1)}, bf16[2,2,64,512]{3,2,1,0:T(8,128)(2,1)S(1)}, bf16[2,2,64,512]{3,2,1,0:T(8,128)(2,1)S(1)}, bf16[2,2,64,512]{3,2,1,0:T(8,128)(2,1)S(1)}) custom-call(bf16[64,2048]{1,0:T(8,128)(2,1)S(1)} %copy-done, bf16[64,2048]{1,0:T(8,128)(2,1)S(1)} %copy-done.1, bf16[64,2048]{1,0:T(8,128)(2,1)S(1)} %copy-done.2, ...), custom_call_target="tpu_custom_call" | custom-call | flops 3221225472 | bytes 2097152 | tf_op jit(solution)/shard_map/pallas_call | solution.py:454
  74.4 0.7 copy.14
  75.1 0.7 copy.15
  75.8 0.7 copy.16
  76.5 0.7 copy.17
Async XLA Ops:
  0.6 1.0 %copy-start = (bf16[64,2048]{1,0:T(8,128)(2,1)S(1)}, bf16[64,2048]{1,0:T(8,128)(2,1)}, u32[]{:S(2)}) copy-start(bf16[64,2048]{1,0:T(8,128)(2,1)} %k_ref.1) | copy-start | bytes 786436
  1.6 0.9 %copy-start.1 = (bf16[64,2048]{1,0:T(8,128)(2,1)S(1)}, bf16[64,2048]{1,0:T(8,128)(2,1)}, u32[]{:S(2)}) copy-start(bf16[64,2048]{1,0:T(8,128)(2,1)} %q_ref.1) | copy-start | bytes 786436
  2.5 0.9 %copy-start.2 = (bf16[64,2048]{1,0:T(8,128)(2,1)S(1)}, bf16[64,2048]{1,0:T(8,128)(2,1)}, u32[]{:S(2)}) copy-start(bf16[64,2048]{1,0:T(8,128)(2,1)} %v_ref.1) | copy-start | bytes 786436
  3.5 0.9 %copy-start.3 = (bf16[64,2048]{1,0:T(8,128)(2,1)S(1)}, bf16[64,2048]{1,0:T(8,128)(2,1)}, u32[]{:S(2)}) copy-start(bf16[64,2048]{1,0:T(8,128)(2,1)} %g_ref.1) | copy-start | bytes 786436
  4.4 0.7 copy-start.4
  5.1 0.7 copy-start.5

commit v2 on v1

--- a/solution.py
+++ b/solution.py
@@ -219,7 +219,7 @@
     seq, heads, per_out,
     k_ref, q_ref, v_ref, g_ref, random_ref, global_ref,
     out_ref, dq_ref, dk_ref, dv_ref,
-    kb, qb, vb, gb, cb, bias, dka, dva, dkr, dvr, stage,
+    kb, qb, vb, gb, cb, bias, probs, dka, dva, dkr, dvr, stage,
     send_sem, recv_sem, own_sem, swap_send, swap_recv, grad_send, grad_recv,
     out_send, out_recv,
 ):
@@ -288,18 +288,22 @@
     ]
     for a in range(4):
         own[a].start()
-    for group in ((0, 4, 1), (2, 3)):
-        @pl.loop(1, chips)
-        def _(j):
-            for a in group:
-                block_copy(a, j).start()
+    parts = chips // GROUP
+    part = place // GROUP
+
+    for group in ((0, 4), (1,), (3,), (2,)):
+        for first, last in ((chips // 2, chips), (1, chips // 2)):
+            @pl.loop(first, last)
+            def _(j):
+                for a in group:
+                    block_copy(a, j).start()
     for a in range(4):
         own[a].wait()
 
-    def swap(n, part):
-        ref = (kb, vb)[n].at[part]
+    def swap(n, core, m):
+        ref = (kb, vb)[n].at[core, pl.ds(m * GROUP, GROUP)]
         return pltpu.make_async_remote_copy(
-            src_ref=ref, dst_ref=ref, send_sem=swap_send.at[n], recv_sem=swap_recv.at[n],
+            src_ref=ref, dst_ref=ref, send_sem=swap_send.at[n, m], recv_sem=swap_recv.at[n, m],
             device_id=sibling, device_id_type=MESH,
         )
 
@@ -308,10 +312,24 @@
         def _(j):
             arrival(a, (place + j) % chips).wait_recv()
 
-    arrive(0)
-    swap(0, c).start()
+    def arrive_and_swap(a, n):
+        @pl.loop(0, parts)
+        def _(v):
+            m = (part + parts // 2 + parts - v) % parts
+            for d in range(GROUP):
+                @pl.when(m * GROUP + d != place)
+                def _():
+                    arrival(a, m * GROUP + d).wait_recv()
+
+            swap(n, c, m).start()
+
+    def swapped(n):
+        @pl.loop(0, parts)
+        def _(m):
+            swap(n, 1 - c, m).wait_recv()
+
+    arrive_and_swap(0, 0)
     arrive(4)
-    arrive(1)
 
     rows = lax.broadcasted_iota(jnp.int32, (8 * chips, chips * BLOCK_TOKENS), 0)
     cols = lax.broadcasted_iota(jnp.int32, (8 * chips, chips * BLOCK_TOKENS), 1)
@@ -322,39 +340,29 @@
     for u in range(chips // GROUP):
         bias[u] = logs[:, u * width : (u + 1) * width]
 
-    arrive(2)
-    swap(1, c).start()
-    arrive(3)
     dka[...] = jnp.zeros_like(dka)
     dva[...] = jnp.zeros_like(dva)
-    swap(0, 1 - c).wait_recv()
-    swap(1, 1 - c).wait_recv()
+    arrive(1)
+    swapped(0)
 
     total = 2 * chips * BLOCK_TOKENS
     scale = 1.0 / math.sqrt(HEAD_SIZE)
 
-    @pl.loop(0, chips // GROUP)
+    @pl.loop(0, parts)
     def _(u):
-        picked = pl.ds(u * GROUP, GROUP)
         keys = kb[...].reshape(total, HEAD_SIZE)
-        values = vb[...].reshape(total, HEAD_SIZE)
-        query = qb[picked].reshape(width, HEAD_SIZE)
-        cotan = gb[picked].reshape(width, HEAD_SIZE)
+        query = qb[pl.ds(u * GROUP, GROUP)].reshape(width, HEAD_SIZE)
         score = contract(keys, query, 1, 1).reshape(2 * chips, BLOCK_TOKENS, width)
         score = (score * scale + bias[u][:, None, :]).reshape(total, width)
         power = jnp.exp(score - jnp.max(score, axis=0, keepdims=True))
-        prob = power * (1.0 / jnp.sum(power, axis=0, keepdims=True))
-        low = prob.astype(jnp.bfloat16)
-        dprob = contract(values, cotan, 1, 1)
-        delta = jnp.sum(prob * dprob, axis=0, keepdims=True)
-        dscore = (prob * (dprob - delta) * scale).astype(jnp.bfloat16)
-        attended = contract(low, values, 0, 0)
-        dquery = contract(dscore, keys, 0, 0)
-        halves = (GROUP // planes, planes, BLOCK_TOKENS, HEAD_SIZE)
-        slot = pl.ds(u * (GROUP // planes), GROUP // planes)
-        stage[0, slot] = attended.astype(jnp.bfloat16).reshape(halves)
-        stage[1, slot] = dquery.astype(jnp.bfloat16).reshape(halves)
-        dka[...] += contract(dscore, query, 1, 0).reshape(dka.shape)
+        probs[u] = power * (1.0 / jnp.sum(power, axis=0, keepdims=True))
+
+    arrive(3)
+
+    @pl.loop(0, parts)
+    def _(u):
+        cotan = gb[pl.ds(u * GROUP, GROUP)].reshape(width, HEAD_SIZE)
+        low = probs[u].astype(jnp.bfloat16)
         dva[...] += contract(low, cotan, 1, 0).reshape(dva.shape)
 
     def grad_copy(n):
@@ -364,7 +372,6 @@
             device_id=sibling, device_id_type=MESH,
         )
 
-    grad_copy(0).start()
     grad_copy(1).start()
 
     results = (out_ref, dq_ref, dk_ref, dv_ref)
@@ -384,48 +391,78 @@
             stage.at[a, s], results[a].at[:, c, :, lanes], own_sem.at[a]
         )
 
-    keep = out_core == c
-
-    def send_out(a):
-        @pl.loop(1, seq)
-        def _(j):
-            out_copy(a, (s + j) % seq).start()
-
-        @pl.when(keep)
+    def stays(t):
+        return (out_core == c) & (t == s)
+
+    def send_out(a, t):
+        @pl.when(stays(t))
         def _():
             out_own(a).start()
 
-        @pl.when(jnp.logical_not(keep))
+        @pl.when(jnp.logical_not(stays(t)))
         def _():
-            out_copy(a, s).start()
-
-    send_out(0)
-    send_out(1)
-    for n in range(2):
+            out_copy(a, t).start()
+
+    def send_grad(n):
         grad_copy(n).wait_recv()
         final = (dka, dva)[n][c] + (dkr, dvr)[n][...]
         stage[2 + n] = final.astype(jnp.bfloat16).reshape(stage.shape[1:])
-        send_out(2 + n)
+
+        @pl.loop(0, seq)
+        def _(j):
+            send_out(2 + n, (s + seq // 2 + j) % seq)
+
+    arrive_and_swap(2, 1)
+    send_grad(1)
+    swapped(1)
+    shards_each = GROUP // planes
+
+    @pl.loop(0, parts)
+    def _(v):
+        u = (part + parts // 2 + v) % parts
+        keys = kb[...].reshape(total, HEAD_SIZE)
+        values = vb[...].reshape(total, HEAD_SIZE)
+        query = qb[pl.ds(u * GROUP, GROUP)].reshape(width, HEAD_SIZE)
+        cotan = gb[pl.ds(u * GROUP, GROUP)].reshape(width, HEAD_SIZE)
+        prob = probs[u]
+        halves = (shards_each, planes, BLOCK_TOKENS, HEAD_SIZE)
+        slot = pl.ds(u * shards_each, shards_each)
+        attended = contract(prob.astype(jnp.bfloat16), values, 0, 0)
+        stage[0, slot] = attended.astype(jnp.bfloat16).reshape(halves)
+        for d in range(shards_each):
+            send_out(0, u * shards_each + d)
+        dprob = contract(values, cotan, 1, 1)
+        delta = jnp.sum(prob * dprob, axis=0, keepdims=True)
+        dscore = (prob * (dprob - delta) * scale).astype(jnp.bfloat16)
+        dquery = contract(dscore, keys, 0, 0)
+        stage[1, slot] = dquery.astype(jnp.bfloat16).reshape(halves)
+        for d in range(shards_each):
+            send_out(1, u * shards_each + d)
+        dka[...] += contract(dscore, query, 1, 0).reshape(dka.shape)
+
+    grad_copy(0).start()
+    send_grad(0)
 
     for a in range(5):
         @pl.loop(1, chips)
         def _(j):
             block_copy(a, j).wait_send()
     for n in range(2):
-        swap(n, c).wait_send()
+        @pl.loop(0, parts)
+        def _(m):
+            swap(n, c, m).wait_send()
+
         grad_copy(n).wait_send()
     for a in range(4):
-        @pl.loop(1, seq)
-        def _(j):
-            out_copy(a, (s + j) % seq).wait_send()
-
-        @pl.when(keep)
-        def _():
-            out_own(a).wait()
-
-        @pl.when(jnp.logical_not(keep))
-        def _():
-            out_copy(a, s).wait_send()
+        @pl.loop(0, seq)
+        def _(t):
+            @pl.when(stays(t))
+            def _():
+                out_own(a).wait()
+
+            @pl.when(jnp.logical_not(stays(t)))
+            def _():
+                out_copy(a, t).wait_send()
 
         for d in range(per_out):
             for core in range(2):
@@ -464,6 +501,7 @@
             pltpu.VMEM(blocks, low),
             pltpu.VMEM((chips, 8, 128), wide),
             pltpu.VMEM((chips // GROUP, 2 * chips, GROUP * rows), wide),
+            pltpu.VMEM((chips // GROUP, 2 * half, GROUP * rows), wide),
             pltpu.VMEM((2, half, HEAD_SIZE), wide),
             pltpu.VMEM((2, half, HEAD_SIZE), wide),
             pltpu.VMEM((half, HEAD_SIZE), wide),
@@ -472,15 +510,15 @@
             dma((5, chips)),
             dma((5, chips)),
             dma((4,)),
-            dma((2,)),
-            dma((2,)),
+            dma((2, chips // GROUP)),
+            dma((2, chips // GROUP)),
             dma((2,)),
             dma((2,)),
             dma((4, seq)),
             dma((4, per_out, 2)),
         ],
         compiler_params=pltpu.CompilerParams(
-            collective_id=0, has_side_effects=True, vmem_limit_bytes=48 * 2**20
+            collective_id=0, has_side_effects=True, vmem_limit_bytes=63 * 2**20
         ),
         cost_estimate=pl.CostEstimate(
             flops=flops, bytes_accessed=16 * rows * feat, transcendentals=2 * half * half

time: 78.6 us -> 67.8 us (0.86)
  the two profiles are of different devices: /device:TPU:11 before, /device:TPU:1 now
where the time goes in v2:
time: 67.8 us; the launch traced here: 67.6 us
  Pallas kernels  62.4 us (92%)
  local copies, waits for them, and re-layouts  4.5 us (7%)
    pallas_call x1, Pallas kernels, by_head(): pl.pallas_call(functools.partial(head_kernel, seq, heads, per_out), out_s...  62.4 us
    unnamed x10, local copies, waits for them, and re-layouts  4.5 us

profile of v2, /device:TPU:1, one launch (start us, length us, event | category | flops | bytes accessed | tf_op | source)
XLA Modules:
  0.0 67.6 jit_solution(1824938437058802984)
XLA Ops:
  0.6 62.4 %shard_map.93 = (bf16[2,2,64,512]{3,2,1,0:T(8,128)(2,1)}, bf16[2,2,64,512]{3,2,1,0:T(8,128)(2,1)}, bf16[2,2,64,512]{3,2,1,0:T(8,128)(2,1)}, bf16[2,2,64,512]{3,2,1,0:T(8,128)(2,1)}) custom-call(bf16[64,2048]{1,0:T(8,128)(2,1)} %k_ref.1, bf16[64,2048]{1,0:T(8,128)(2,1)} %q_ref.1, bf16[64,2048]{1,0:T(8,128)(2,1)} %v_ref.1, bf16[64,2048]{1,0:T(8,128)(2,1)} %g_ref.1, ...), custom_call_target="tpu_custom_call" | custom-call | flops 3221225472 | bytes 2097152 | tf_op jit(solution)/shard_map/pallas_call | solution.py:491
  63.1 0.0 copy-start.2
  63.1 1.7 %copy.14 = bf16[256,512]{1,0:T(8,128)(2,1)} copy(bf16[256,512]{1,0:T(8,128)(2,1)} %bitcast.7) | data formatting | bytes 524288
  64.8 0.0 copy-done.2
  64.8 0.0 copy-start.1
  64.8 0.7 %copy.15 = bf16[256,512]{1,0:T(8,128)(2,1)} copy(bf16[256,512]{1,0:T(8,128)(2,1)S(1)} %bitcast.6) | data formatting | bytes 524288
  65.5 0.3 copy-done.1
  65.9 0.0 copy-start
  65.9 0.7 %copy.16 = bf16[256,512]{1,0:T(8,128)(2,1)} copy(bf16[256,512]{1,0:T(8,128)(2,1)S(1)} %bitcast.5) | data formatting | bytes 524288
  66.6 0.3 copy-done
  66.9 0.7 %copy.17 = bf16[256,512]{1,0:T(8,128)(2,1)} copy(bf16[256,512]{1,0:T(8,128)(2,1)S(1)} %bitcast.4) | data formatting | bytes 524288
Async XLA Ops:
  63.1 1.7 %copy-start.2 = (bf16[2,2,64,512]{3,2,1,0:T(8,128)(2,1)S(1)}, bf16[2,2,64,512]{3,2,1,0:T(8,128)(2,1)}, u32[]{:S(2)}) copy-start(bf16[2,2,64,512]{3,2,1,0:T(8,128)(2,1)} %get-tuple-element.9) | copy-start | bytes 786436
  64.8 1.0 %copy-start.1 = (bf16[2,2,64,512]{3,2,1,0:T(8,128)(2,1)S(1)}, bf16[2,2,64,512]{3,2,1,0:T(8,128)(2,1)}, u32[]{:S(2)}) copy-start(bf16[2,2,64,512]{3,2,1,0:T(8,128)(2,1)} %get-tuple-element.10) | copy-start | bytes 786436
  65.9 1.0 %copy-start = (bf16[2,2,64,512]{3,2,1,0:T(8,128)(2,1)S(1)}, bf16[2,2,64,512]{3,2,1,0:T(8,128)(2,1)}, u32[]{:S(2)}) copy-start(bf16[2,2,64,512]{3,2,1,0:T(8,128)(2,1)} %get-tuple-element.11) | copy-start | bytes 786436

commit v3 on v2

--- a/solution.py
+++ b/solution.py
@@ -220,7 +220,7 @@
     k_ref, q_ref, v_ref, g_ref, random_ref, global_ref,
     out_ref, dq_ref, dk_ref, dv_ref,
     kb, qb, vb, gb, cb, bias, probs, dka, dva, dkr, dvr, stage,
-    send_sem, recv_sem, own_sem, swap_send, swap_recv, grad_send, grad_recv,
+    kin, qin, vin, gin, send_sem, recv_sem, own_sem, swap_send, swap_recv, grad_send, grad_recv,
     out_send, out_recv,
 ):
     s = lax.axis_index("seq")
@@ -231,7 +231,13 @@
     devices = seq * heads
     me = s * heads + h
     place = s * planes + x
-    sources = (k_ref, q_ref, v_ref, g_ref)
+    sources = (kin, qin, vin, gin)
+    loads = [
+        pltpu.make_async_copy(ref, sources[a], own_sem.at[a])
+        for a, ref in enumerate((k_ref, q_ref, v_ref, g_ref))
+    ]
+    for load in loads:
+        load.start()
     landing = (kb.at[c], qb, vb.at[c], gb)
     sibling = (s, 2 * x + 1 - c)
 
@@ -256,6 +262,8 @@
         count = count + jnp.where(block == entry, 1.0, 0.0)
     cb[place] = count
 
+    for load in loads:
+        load.wait()
     pl.semaphore_wait(barrier, devices - 1)
 
     def columns(to_s, to_x):
@@ -292,11 +300,10 @@
     part = place // GROUP
 
     for group in ((0, 4), (1,), (3,), (2,)):
-        for first, last in ((chips // 2, chips), (1, chips // 2)):
-            @pl.loop(first, last)
-            def _(j):
-                for a in group:
-                    block_copy(a, j).start()
+        @pl.loop(1, chips)
+        def _(j):
+            for a in group:
+                block_copy(a, j).start()
     for a in range(4):
         own[a].wait()
 
@@ -410,7 +417,7 @@
 
         @pl.loop(0, seq)
         def _(j):
-            send_out(2 + n, (s + seq // 2 + j) % seq)
+            send_out(2 + n, (s + 3 + 3 * j) % seq)
 
     arrive_and_swap(2, 1)
     send_grad(1)
@@ -419,7 +426,7 @@
 
     @pl.loop(0, parts)
     def _(v):
-        u = (part + parts // 2 + v) % parts
+        u = (part + 1 + v) % parts
         keys = kb[...].reshape(total, HEAD_SIZE)
         values = vb[...].reshape(total, HEAD_SIZE)
         query = qb[pl.ds(u * GROUP, GROUP)].reshape(width, HEAD_SIZE)
@@ -507,6 +514,10 @@
             pltpu.VMEM((half, HEAD_SIZE), wide),
             pltpu.VMEM((half, HEAD_SIZE), wide),
             pltpu.VMEM((4, seq, planes, rows, HEAD_SIZE), low),
+            pltpu.VMEM((rows, feat), low),
+            pltpu.VMEM((rows, feat), low),
+            pltpu.VMEM((rows, feat), low),
+            pltpu.VMEM((rows, feat), low),
             dma((5, chips)),
             dma((5, chips)),
             dma((4,)),

time: 67.8 us -> 64.3 us (0.948)
  the two profiles are of different devices: /device:TPU:1 before, /device:TPU:11 now
where the time goes in v3:
time: 64.3 us; the launch traced here: 64 us
  Pallas kernels  58.9 us (92%)
  local copies, waits for them, and re-layouts  4.5 us (7%)
  between operations  0.65 us (1%)
    pallas_call x1, Pallas kernels, by_head(): pl.pallas_call(functools.partial(head_kernel, seq, heads, per_out), out_s...  58.9 us
    unnamed x10, local copies, waits for them, and re-layouts  4.5 us

profile of v3, /device:TPU:11, one launch (start us, length us, event | category | flops | bytes accessed | tf_op | source)
XLA Modules:
  0.0 64.0 jit_solution(4797435636313509000)
XLA Ops:
  0.6 58.9 %shard_map.93 = (bf16[2,2,64,512]{3,2,1,0:T(8,128)(2,1)}, bf16[2,2,64,512]{3,2,1,0:T(8,128)(2,1)}, bf16[2,2,64,512]{3,2,1,0:T(8,128)(2,1)}, bf16[2,2,64,512]{3,2,1,0:T(8,128)(2,1)}) custom-call(bf16[64,2048]{1,0:T(8,128)(2,1)} %k_ref.1, bf16[64,2048]{1,0:T(8,128)(2,1)} %q_ref.1, bf16[64,2048]{1,0:T(8,128)(2,1)} %v_ref.1, bf16[64,2048]{1,0:T(8,128)(2,1)} %g_ref.1, ...), custom_call_target="tpu_custom_call" | custom-call | flops 3221225472 | bytes 2097152 | tf_op jit(solution)/shard_map/pallas_call | solution.py:498
  59.5 0.0 copy-start.2
  59.5 1.7 %copy.14 = bf16[256,512]{1,0:T(8,128)(2,1)} copy(bf16[256,512]{1,0:T(8,128)(2,1)} %bitcast.7) | data formatting | bytes 524288
  61.2 0.0 copy-done.2
  61.2 0.0 copy-start.1
  61.2 0.7 %copy.15 = bf16[256,512]{1,0:T(8,128)(2,1)} copy(bf16[256,512]{1,0:T(8,128)(2,1)S(1)} %bitcast.6) | data formatting | bytes 524288
  62.0 0.3 copy-done.1
  62.3 0.0 copy-start
  62.3 0.7 %copy.16 = bf16[256,512]{1,0:T(8,128)(2,1)} copy(bf16[256,512]{1,0:T(8,128)(2,1)S(1)} %bitcast.5) | data formatting | bytes 524288
  63.0 0.3 copy-done
  63.3 0.7 %copy.17 = bf16[256,512]{1,0:T(8,128)(2,1)} copy(bf16[256,512]{1,0:T(8,128)(2,1)S(1)} %bitcast.4) | data formatting | bytes 524288
Async XLA Ops:
  59.5 1.7 %copy-start.2 = (bf16[2,2,64,512]{3,2,1,0:T(8,128)(2,1)S(1)}, bf16[2,2,64,512]{3,2,1,0:T(8,128)(2,1)}, u32[]{:S(2)}) copy-start(bf16[2,2,64,512]{3,2,1,0:T(8,128)(2,1)} %get-tuple-element.9) | copy-start | bytes 786436
  61.2 1.0 %copy-start.1 = (bf16[2,2,64,512]{3,2,1,0:T(8,128)(2,1)S(1)}, bf16[2,2,64,512]{3,2,1,0:T(8,128)(2,1)}, u32[]{:S(2)}) copy-start(bf16[2,2,64,512]{3,2,1,0:T(8,128)(2,1)} %get-tuple-element.10) | copy-start | bytes 786436
  62.3 1.0 %copy-start = (bf16[2,2,64,512]{3,2,1,0:T(8,128)(2,1)S(1)}, bf16[2,2,64,512]{3,2,1,0:T(8,128)(2,1)}, u32[]{:S(2)}) copy-start(bf16[2,2,64,512]{3,2,1,0:T(8,128)(2,1)} %get-tuple-element.11) | copy-start | bytes 786436

commit v4 on v3

--- a/solution.py
+++ b/solution.py
@@ -218,7 +218,7 @@
 def head_kernel(
     seq, heads, per_out,
     k_ref, q_ref, v_ref, g_ref, random_ref, global_ref,
-    out_ref, dq_ref, dk_ref, dv_ref,
+    out_ref,
     kb, qb, vb, gb, cb, bias, probs, dka, dva, dkr, dvr, stage,
     kin, qin, vin, gin, send_sem, recv_sem, own_sem, swap_send, swap_recv, grad_send, grad_recv,
     out_send, out_recv,
@@ -381,7 +381,7 @@
 
     grad_copy(1).start()
 
-    results = (out_ref, dq_ref, dk_ref, dv_ref)
+    results = tuple(out_ref.at[a] for a in range(4))
     out_core, out_slot = s // per_out, s % per_out
 
     def out_copy(a, t):
@@ -492,15 +492,15 @@
     half = chips * rows
     low, wide = jnp.bfloat16, jnp.float32
     dma = pltpu.SemaphoreType.DMA
-    shape = jax.ShapeDtypeStruct((planes, 2, rows, per_out * HEAD_SIZE), low)
+    shape = jax.ShapeDtypeStruct((4, planes, 2, rows, per_out * HEAD_SIZE), low)
     blocks = (chips, rows, HEAD_SIZE)
     flops = 6 * 2 * half * 2 * half * HEAD_SIZE
     results = pl.pallas_call(
         functools.partial(head_kernel, seq, heads, per_out),
-        out_shape=[shape] * 4,
+        out_shape=shape,
         in_specs=[pl.BlockSpec(memory_space=pl.ANY)] * 4
         + [pl.BlockSpec(memory_space=pltpu.SMEM)] * 2,
-        out_specs=[pl.BlockSpec(memory_space=pl.ANY)] * 4,
+        out_specs=pl.BlockSpec(memory_space=pl.ANY),
         scratch_shapes=[
             pltpu.VMEM((2,) + blocks, low),
             pltpu.VMEM(blocks, low),

time: 64.3 us -> 61.9 us (0.963)
  local copies, waits for them, and re-layouts: 4.5 us -> 2.17 us
    unnamed x10 -> x0, local copies, waits for them, and re-layouts: 4.5 us -> none
    another operation x0 -> x1, local copies, waits for them, and re-layouts: none -> 2.17 us  [by_head(): return tuple((r.reshape(2 * planes * rows, per_out * HEAD_SIZE) for r in...]
where the time goes in v4:
time: 61.9 us; the launch traced here: 61.7 us
  Pallas kernels  58.9 us (95%)
  local copies, waits for them, and re-layouts  2.17 us (4%)
  between operations  0.64 us (1%)
    pallas_call x1, Pallas kernels, by_head(): pl.pallas_call(functools.partial(head_kernel, seq, heads, per_out), out_s...  58.9 us
    another operation x1, local copies, waits for them, and re-layouts, by_head(): return tuple((r.reshape(2 * planes * rows, per_out * HEAD_SIZE) for r in...  2.17 us

profile of v4, /device:TPU:11, one launch (start us, length us, event | category | flops | bytes accessed | tf_op | source)
XLA Modules:
  0.0 61.7 jit_solution(6703039145188849377)
XLA Ops:
  0.6 58.9 %shard_map.93 = bf16[4,2,2,64,512]{4,3,2,1,0:T(8,128)(2,1)} custom-call(bf16[64,2048]{1,0:T(8,128)(2,1)} %k_ref.1, bf16[64,2048]{1,0:T(8,128)(2,1)} %q_ref.1, bf16[64,2048]{1,0:T(8,128)(2,1)} %v_ref.1, bf16[64,2048]{1,0:T(8,128)(2,1)} %g_ref.1, s32[4,3]{1,0:T(4,128)} %random_ref.1, s32[2]{0:T(128)} %global_ref.1), custom_call_target="tpu_custom_call" | custom-call | flops 3221225472 | bytes 2097152 | tf_op jit(solution)/shard_map/pallas_call | solution.py:498
  59.5 2.2 %fusion = (bf16[1,2,2,64,512]{4,3,2,1,0:T(8,128)(2,1)}, bf16[1,2,2,64,512]{4,3,2,1,0:T(8,128)(2,1)}, bf16[1,2,2,64,512]{4,3,2,1,0:T(8,128)(2,1)}, bf16[1,2,2,64,512]{4,3,2,1,0:T(8,128)(2,1)}) fusion(bf16[4,2,2,64,512]{4,3,2,1,0:T(8,128)(2,1)} %shard_map.93), kind=kLoop, calls=%fused_computation | loop fusion | bytes 2097152 | tf_op jit(solution)/shard_map/unstack | solution.py:538
